TPU v7x, 768 devices: a whole 4x8x12 slice. The times are simulated.
768 devices in a mesh: wide: 16 (over x_lo, y), narrow: 48 (over x_hi, z, core).
Axes of the slice: x: 4 (x_hi: 2, x_lo: 2; x = x_hi * 2 + x_lo), y: 8, z: 12, core: 2. Of those that a mesh axis runs over, the one named last changes fastest.
Arguments:
- features: bfloat16 [48, 2048, 128], P('narrow', 'wide'), may hold values from -6 to 6
- in_weight: bfloat16 [128, 256], replicated, may hold values from -0.5 to 0.5
- hidden_bias: float32 [256], replicated, may hold values from -4 to 4
- classifier: bfloat16 [256, 172], replicated
- adjacency_tiles: bfloat16 [768, 48, 2, 128, 128], P('wide', 'narrow'), may hold values from -0.375 to 0.375
- tile_col: int32 [768, 48, 2], P('wide', 'narrow'), may hold values from 0 to 15, as said below
- tile_count: int32 [768, 48], P('wide', 'narrow'), may hold values from 1 to 2, as said below
- node_perm: int32 [48, 2048], P('narrow', 'wide'), may hold values from 0 to 2047, as said below
- labels: int32 [98304], P(('wide', 'narrow')), may hold values from 0 to 171
Outputs:
- next_input: bfloat16 [48, 2048, 256], P('narrow', 'wide')
- node_loss: float32 [98304], P(('wide', 'narrow'))
- input_grad: float32 [48, 2048, 128], P('narrow', 'wide')
Inputs may be any that keep to these rules, and one draw needn't show every extreme that they name: `tile_col`: within one block row and one column group the 2 entries are distinct. `tile_count`: on every device one of its block rows has all 2 slots live. `node_perm`: each row is a permutation of 0 to 2047; of the 128 entries from j * 128 to (j + 1) * 128 - 1, at most 12 lie in any one range d * 128 to (d + 1) * 128 - 1, and exactly 12 in some range.
All inputs are finite; a program needn't handle non-finite values.
Results may differ from a plain program's by a relative error of at most 0.023.
Values may be sent and summed in bfloat16 or wider, within the bound.
A program may use at most 64 MiB of HBM per device.

v0:
```python
import jax
import jax.numpy as jnp
from jax import lax
from jax.sharding import PartitionSpec as P

finest = lax.Precision.HIGHEST


def score_nodes(hidden_pre, classifier, labels):
    gate_value = jax.nn.sigmoid(hidden_pre)
    activated = (hidden_pre * gate_value).astype(jnp.bfloat16)
    logits = jnp.dot(activated, classifier, preferred_element_type=jnp.float32)
    top_score = jnp.max(logits, axis=1, keepdims=True)
    shifted = jnp.exp(logits - top_score)
    exp_total = jnp.sum(shifted, axis=1, keepdims=True)
    target = labels[:, None] == jnp.arange(logits.shape[1])[None, :]
    picked = jnp.sum(jnp.where(target, logits, jnp.zeros_like(logits)), axis=1)
    node_loss = top_score[:, 0] + jnp.log(exp_total[:, 0]) - picked
    grad_logits = shifted / exp_total - target.astype(jnp.float32)
    grad_act = jnp.dot(grad_logits, classifier.astype(jnp.float32).T, precision=finest)
    grad_pre = (grad_act * gate_value * (1.0 + hidden_pre * (1.0 - gate_value))).astype(
        jnp.bfloat16
    )
    return (activated, node_loss, grad_pre)


def gather_blocks(blocks, columns, live_slots, source):
    row_blocks, tile_slots, tile_edge = (blocks.shape[0], blocks.shape[1], blocks.shape[2])
    width = source.shape[1]
    grouped = source.reshape(-1, tile_edge, width)
    total = jnp.zeros((row_blocks, tile_edge, width), jnp.float32)
    for slot_index in range(tile_slots):
        chosen = grouped[columns[:, slot_index]]
        product = jnp.einsum(
            "bik,bkf->bif", blocks[:, slot_index], chosen, preferred_element_type=jnp.float32
        )
        total = total + jnp.where(live_slots[:, slot_index, None, None], product, 0.0)
    return total.reshape(row_blocks * tile_edge, width)


def spread_blocks(blocks, columns, live_slots, rows, col_blocks):
    row_blocks, tile_slots, tile_edge = (blocks.shape[0], blocks.shape[1], blocks.shape[2])
    width = rows.shape[1]
    grouped = rows.reshape(row_blocks, tile_edge, width)
    upper = grouped.astype(jnp.bfloat16)
    lower = (grouped - upper.astype(jnp.float32)).astype(jnp.bfloat16)
    total = jnp.zeros((col_blocks, tile_edge, width), jnp.float32)
    for slot_index in range(tile_slots):
        tiles = blocks[:, slot_index]
        part = jnp.einsum("bik,bif->bkf", tiles, upper, preferred_element_type=jnp.float32)
        part = part + jnp.einsum("bik,bif->bkf", tiles, lower, preferred_element_type=jnp.float32)
        part = jnp.where(live_slots[:, slot_index, None, None], part, 0.0)
        total = total.at[columns[:, slot_index]].add(part)
    return total.reshape(col_blocks * tile_edge, width)


def per_device(
    features,
    in_weight,
    hidden_bias,
    classifier,
    adjacency_tiles,
    tile_col,
    tile_count,
    node_perm,
    labels,
):
    own_rows = features.reshape(features.shape[1], features.shape[2])
    node_count = own_rows.shape[0]
    wide_size = lax.axis_size("wide")
    row_blocks, tile_slots, tile_edge = (
        adjacency_tiles.shape[0],
        adjacency_tiles.shape[2],
        adjacency_tiles.shape[3],
    )
    col_blocks = node_count * wide_size // tile_edge
    blocks = adjacency_tiles.reshape(row_blocks, tile_slots, tile_edge, tile_edge)
    columns = tile_col.reshape(row_blocks, tile_slots)
    live_slots = jnp.arange(tile_slots)[None, :] < tile_count
    weight_wide = in_weight.astype(jnp.float32)
    group_rows = lax.all_gather(own_rows, "wide", axis=0, tiled=True)
    partial_sums = gather_blocks(blocks, columns, live_slots, group_rows)
    aggregated = lax.psum_scatter(partial_sums, "narrow", scatter_dimension=0, tiled=True)
    hidden_pre = jnp.dot(aggregated, weight_wide, precision=finest) + hidden_bias
    activated, node_loss, grad_pre = score_nodes(hidden_pre, classifier, labels)
    backward_rows = jnp.dot(grad_pre.astype(jnp.float32), weight_wide.T, precision=finest)
    grad_rows = lax.all_gather(
        backward_rows.astype(jnp.bfloat16), "narrow", axis=0, tiled=True
    ).astype(backward_rows.dtype)
    column_terms = spread_blocks(blocks, columns, live_slots, grad_rows, col_blocks)
    input_grad = lax.psum_scatter(
        column_terms.astype(jnp.bfloat16), "wide", scatter_dimension=0, tiled=True
    ).astype(jnp.float32)
    targets = node_perm.reshape(node_count)
    my_positions = lax.axis_index("wide") * node_count + jnp.arange(node_count)
    every_row, every_target = (
        lax.all_gather(activated, "wide", axis=0, tiled=True),
        lax.all_gather(targets, "wide", axis=0, tiled=True),
    )
    placing = (every_target[None, :] == my_positions[:, None]).astype(jnp.bfloat16)
    next_rows = jnp.dot(placing, every_row, preferred_element_type=jnp.float32).astype(jnp.bfloat16)
    return (next_rows.reshape(1, node_count, -1), node_loss, input_grad.reshape(1, node_count, -1))


def solution(mesh):
    in_specs = (
        P("narrow", "wide", None),
        P(),
        P(),
        P(),
        P("wide", "narrow", None, None, None),
        P("wide", "narrow", None),
        P("wide", "narrow"),
        P("narrow", "wide"),
        P(("wide", "narrow")),
    )
    out_specs = (P("narrow", "wide", None), P(("wide", "narrow")), P("narrow", "wide", None))
    return jax.shard_map(
        per_device, mesh=mesh, in_specs=in_specs, out_specs=out_specs, check_vma=False
    )
```

profile of v0, /device:TPU:6, one launch (start us, length us, event | category | flops | bytes accessed | tf_op | source)
XLA Modules:
  0.0 517.4 jit_solution(4271072821738036483)
XLA Ops:
  7.2 0.0 copy-start
  7.2 0.0 reduce-scatter.3.cloned.1.call-start
  7.2 38.7 %all-gather.1 = bf16[1,2048,128]{2,1,0:T(8,128)(2,1)} all-gather(bf16[1,128,128]{2,1,0:T(8,128)(2,1)} %param.9), channel_id=3, replica_groups=mesh['wide'=16,'narrow'=48] {'wide'}, dimensions={1}, use_global_device_ids=true | all-gather | bytes 557056 | tf_op jit(solution)/shard_map/all_gather | solution.py:81
  45.9 0.8 fusion.17
  46.7 2.3 copy.27
  49.0 0.0 copy-start.1
  49.0 0.0 copy-start.11
  49.0 3.5 gather_fusion
  52.5 3.0 gather_fusion.1
  55.5 0.0 copy-start.5
  55.5 2.1 fusion.1
  57.6 0.0 copy-done.5
  57.6 2.3 select_add_fusion
  60.0 0.0 reduce-scatter.3.cloned.1.call-update
  60.0 0.0 all-gather.7.cloned.1.call-start
  60.1 181.1 %reduce-scatter.3.cloned.1.call-done = f32[128,128]{1,0:T(8,128)} async-done(((f32[6144,128]{1,0:T(8,128)}), f32[128,128]{1,0:T(8,128)}) %reduce-scatter.3.cloned.1.call-update) | async-done | bytes 65552 | tf_op jit(solution)/shard_map/reduce_scatter | solution.py:83
  241.1 1.1 multiply_convert_fusion
  242.2 0.0 copy-start.6
  242.2 0.2 fusion.18
  242.4 0.0 copy-done.8
  242.4 0.1 fusion.12
  242.5 0.3 fusion.4
  242.8 0.8 convolution_convert_fusion.1
  243.6 0.0 all-gather.7.cloned.1.call-update
  243.6 0.0 all-gather.5.cloned.1.call-start
  243.7 0.0 copy-done.6
  243.7 0.7 all-gather.5.cloned.1.call-update
  244.4 0.0 reduce-scatter.5.cloned.1.call-start
  244.4 114.6 %all-gather.7.cloned.1.call-done = bf16[6144,128]{1,0:T(8,128)(2,1)} async-done(((bf16[128,128]{1,0:T(8,128)(2,1)}), bf16[6144,128]{1,0:T(8,128)(2,1)}) %all-gather.7.cloned.1.call-update) | async-done | bytes 1572880 | tf_op jit(solution)/shard_map/all_gather | solution.py:87
  359.0 2.7 copy.14
  361.7 2.2 fusion
  363.9 2.9 select_bitcast_fusion.1
  366.9 0.1 broadcast_in_dim.54
  367.0 6.7 %scatter_fusion = f32[16,128,128]{2,1,0:T(8,128)S(1)} fusion(f32[16,128,128]{2,1,0:T(8,128)S(1)} %broadcast_in_dim.54, s32[48]{0:T(128)S(1)} %get-tuple-element.6, f32[48,128,128]{2,1,0:T(8,128)} %select_bitcast_fusion.1), kind=kCustom, calls=%fused_computation.2 | custom fusion | flops 786432 | bytes 9437376 | tf_op jit(solution)/shard_map/scatter-add | solution.py:53
  373.7 2.7 fusion.2
  376.4 0.1 copy-done.2
  376.5 0.5 copy-done.4
  377.0 2.9 select_bitcast_fusion
  379.9 6.7 %scatter_fusion.1 = f32[16,128,128]{2,1,0:T(8,128)S(1)} fusion(f32[16,128,128]{2,1,0:T(8,128)S(1)} %scatter_fusion, s32[48]{0:T(128)S(1)} %get-tuple-element.5, f32[48,128,128]{2,1,0:T(8,128)} %select_bitcast_fusion), kind=kCustom, calls=%fused_computation.3 | custom fusion | flops 786432 | bytes 9437376 | tf_op jit(solution)/shard_map/scatter-add | solution.py:53
  386.7 0.9 convert_element_type.38
  387.6 0.0 reduce-scatter.5.cloned.1.call-update
  387.6 0.0 copy-done.9
  387.6 32.2 %all-gather = s32[1,2048]{1,0:T(1,128)S(1)} all-gather(s32[1,128]{1,0:T(1,128)S(1)} %copy-done.9), channel_id=2, replica_groups=mesh['wide'=16,'narrow'=48] {'wide'}, dimensions={1}, use_global_device_ids=true | all-gather | bytes 8704 | tf_op jit(solution)/shard_map/all_gather | solution.py:98
  419.8 0.5 add_subtract_fusion
  420.3 13.2 %all-gather.5.cloned.1.call-done = bf16[2048,256]{1,0:T(8,128)(2,1)} async-done(((bf16[128,256]{1,0:T(8,128)(2,1)}), bf16[2048,256]{1,0:T(8,128)(2,1)}) %all-gather.5.cloned.1.call-update) | async-done | bytes 1048592 | tf_op jit(solution)/shard_map/all_gather | solution.py:97
  433.5 2.2 fusion.5
  435.7 73.8 %reduce-scatter.5.cloned.1.call-done = bf16[128,128]{1,0:T(8,128)(2,1)} async-done(((bf16[2048,128]{1,0:T(8,128)(2,1)}), bf16[128,128]{1,0:T(8,128)(2,1)}) %reduce-scatter.5.cloned.1.call-update) | async-done | bytes 32784 | tf_op jit(solution)/shard_map/reduce_scatter | solution.py:91
  509.5 1.4 bitcast_convert_fusion
  (17 shorter events, 0.0 us)
Async XLA Ops:
  7.2 235.1 %copy-start = (bf16[256,172]{0,1:T(8,128)(2,1)S(1)}, bf16[256,172]{0,1:T(8,128)(2,1)}, u32[]{:S(2)}) copy-start(bf16[256,172]{0,1:T(8,128)(2,1)} %param.12) | copy-start | bytes 264196
  7.2 234.0 %reduce-scatter.3.cloned.1.call-start = ((), (), s32[]{:S(2)}) async-start(), calls=%async_computation.2 | async-start | bytes 3211264 | tf_op jit(solution)/shard_map/reduce_scatter | solution.py:83
  49.0 314.9 %copy-start.1 = (bf16[48,1,2,128,128]{4,3,0,2,1:T(8,128)(2,1)}, bf16[48,1,2,128,128]{4,3,0,2,1:T(8,128)(2,1)S(1)}, u32[]{:S(2)}) copy-start(bf16[48,1,2,128,128]{4,3,0,2,1:T(8,128)(2,1)S(1)} %copy.27) | copy-start | bytes 9437188
  49.0 6.5 %copy-start.11 = (s32[48,1]{0,1:T(1,128)S(1)}, s32[48,1]{0,1:T(1,128)}, u32[]{:S(2)}) copy-start(s32[48,1]{0,1:T(1,128)} %param.15) | copy-start | bytes 580
  55.5 2.1 copy-start.5
  60.0 181.2 %copy-start.7 = (bf16[128,256]{1,0:T(8,128)(2,1)S(1)}, bf16[128,256]{1,0:T(8,128)(2,1)}, u32[]{:S(2)}) copy-start(bf16[128,256]{1,0:T(8,128)(2,1)} %param.10) | copy-start | bytes 196612
  60.0 181.2 %copy-start.10 = (f32[256]{0:T(256)S(1)}, f32[256]{0:T(256)}, u32[]{:S(2)}) copy-start(f32[256]{0:T(256)} %param.11) | copy-start | bytes 3076
  60.0 182.4 %copy-start.8 = (s32[128]{0:T(128)S(1)}, s32[128]{0:T(128)}, u32[]{:S(2)}) copy-start(s32[128]{0:T(128)} %param.17) | copy-start | bytes 1540
  60.0 299.0 %all-gather.7.cloned.1.call-start = ((), (), s32[]{:S(2)}) async-start(), calls=%async_computation.4 | async-start | bytes 1605632 | tf_op jit(solution)/shard_map/all_gather | solution.py:87
  242.2 1.5 copy-start.6
  243.6 189.9 %all-gather.5.cloned.1.call-start = ((), (), s32[]{:S(2)}) async-start(), calls=%async_computation.3 | async-start | bytes 1114112 | tf_op jit(solution)/shard_map/all_gather | solution.py:97
  244.4 265.1 %reduce-scatter.5.cloned.1.call-start = ((), (), s32[]{:S(2)}) async-start(), calls=%async_computation.5 | async-start | bytes 557056 | tf_op jit(solution)/shard_map/reduce_scatter | solution.py:91
  361.7 2.3 copy-start.3
  373.7 2.8 copy-start.2
  373.7 3.3 copy-start.4
  379.9 7.7 %copy-start.9 = (s32[1,128]{1,0:T(1,128)S(1)}, s32[1,128]{1,0:T(1,128)}, u32[]{:S(2)}) copy-start(s32[1,128]{1,0:T(1,128)} %param.16) | copy-start | bytes 1540
Sparse Core Ops, SparseCore 0:
  60.1 180.9 reduce-scatter.2
  245.4 113.5 all-gather.6
  361.9 71.5 all-gather.4
  436.4 72.9 reduce-scatter.4
where the time goes:
time: 518 us; the launch traced here: 517 us
  waiting for transfers between devices  383 us (74%)
  blocking collectives  70.9 us (14%)
  matrix products  19.8 us (4%)
  other arithmetic  17.1 us (3%)
  between operations  14 us (3%)
  local copies, waits for them, and re-layouts  12.1 us (2%)
    reduce_scatter x1, waiting for transfers between devices, per_device(): lax.psum_scatter(partial_sums, 'narrow', scatter_dimension=0, tiled=True)  181 us
    all_gather x1, waiting for transfers between devices, per_device(): lax.all_gather(backward_rows.astype(jnp.bfloat16), 'narrow', axis=0, tile...  115 us
    reduce_scatter x1, waiting for transfers between devices, per_device(): lax.psum_scatter(column_terms.astype(jnp.bfloat16), 'wide', scatter_dimen...  73.8 us
    all_gather x1, blocking collectives, per_device(): group_rows = lax.all_gather(own_rows, 'wide', axis=0, tiled=True)  38.7 us
    all_gather x1, blocking collectives, per_device(): lax.all_gather(targets, 'wide', axis=0, tiled=True)  32.2 us
    scatter-add x2, other arithmetic, spread_blocks(): total = total.at[columns[:, slot_index]].add(part)  13.5 us
    all_gather x1, waiting for transfers between devices, per_device(): lax.all_gather(activated, 'wide', axis=0, tiled=True)  13.2 us
  transfers between devices with their start and end apart: 4, of which 4 were waited for; matrix products, arithmetic and copies ran while one was open for 6% of the time, Pallas kernels for 0%

commit v1 on v0

v1 whole, which is shorter than its diff:
```python
import functools

import jax
import jax.numpy as jnp
from jax import lax
from jax.experimental import pallas as pl
from jax.experimental.pallas import tpu as pltpu
from jax.sharding import PartitionSpec as P

MESH = pl.DeviceIdType.MESH
LAG = 3
f32, bf16 = jnp.float32, jnp.bfloat16


def ring_offset(k, size):
    steps = size // 2 - (k + 1) // 2
    return steps * ((k % 2) * 2 - 1)


def ring_to(place, k, size):
    return (place + size + ring_offset(k, size)) % size


def ring_from(place, k, size):
    return (place + size - ring_offset(k, size)) % size


def dot(a, b, contract):
    return lax.dot_general(a, b, ((contract[:1], contract[1:]), ((), ())), preferred_element_type=f32)


def split_dot(a, b):
    high = b.astype(bf16)
    low = (b - high.astype(f32)).astype(bf16)
    return dot(a, high, (1, 0)) + dot(a, low, (1, 0))


def layer_kernel(
    wide, narrow,
    feat_ref, weight_ref, bias_ref, cls_ref, tiles_hbm, col_ref, count_ref, prev_ref, perm_ref, labels_ref,
    next_ref, loss_ref, grad_ref,
    tiles, ft, sbuf, srecv, xbuf, xrecv, zbuf, zrecv, own, gbuf, run,
    pack, unpack, cxbuf, cxrecv, cybuf, cyrecv, cpad,
    tile_sem, fy_s, fy_r, fx_s, fx_r, s_s, s_r, x_s, x_r, z_s, z_r,
    gz_s, gz_r, gx_s, gx_r, gs_s, gs_r, cx_s, cx_r, cy_s, cy_r, a_s, a_r,
):
    Y, Z = wide // 2, narrow // 4
    w, n = lax.axis_index("wide"), lax.axis_index("narrow")
    xl, y = w // Y, w % Y
    xh, z, c = n // (2 * Z), (n // 2) % Z, n % 2

    def nid(xh_, z_, c_):
        return (xh_ * Z + z_) * 2 + c_

    def rcopy(src, dst, ss, rs, dev):
        return pltpu.make_async_remote_copy(
            src_ref=src, dst_ref=dst, send_sem=ss, recv_sem=rs, device_id=dev, device_id_type=MESH
        )

    x_dev = (w, nid(1 - xh, z, c))
    s_dev = (w, nid(xh, z, 1 - c))
    xl_dev = ((1 - xl) * Y + y, n)

    def z_dev(k):
        return (w, nid(xh, ring_to(z, k, Z), c))

    def y_dev(k):
        return (xl * Y + ring_to(y, k, Y), n)

    barrier = pltpu.get_barrier_semaphore()
    for d in range(1, wide):
        pl.semaphore_signal(barrier, inc=1, device_id=((w + d) % wide, n), device_id_type=MESH)
    for k in range(Z - 1):
        pl.semaphore_signal(barrier, inc=1, device_id=z_dev(k), device_id_type=MESH)
    pl.semaphore_signal(barrier, inc=1, device_id=x_dev, device_id_type=MESH)
    pl.semaphore_signal(barrier, inc=1, device_id=s_dev, device_id_type=MESH)

    tile_copy = pltpu.make_async_copy(tiles_hbm, tiles, tile_sem)
    tile_copy.start()
    ft[w] = feat_ref[...].astype(f32).T.astype(bf16)
    ft[wide] = jnp.zeros_like(ft[wide])
    run[0] = jnp.zeros_like(run[0])

    pl.semaphore_wait(barrier, wide - 1 + Z - 1 + 2)

    def fy(k, slot):
        return rcopy(ft.at[slot], ft.at[slot], fy_s.at[k], fy_r.at[k], y_dev(k))

    def fx(k, slot):
        return rcopy(ft.at[slot], ft.at[slot], fx_s.at[k], fx_r.at[k], xl_dev)

    fx(Y - 1, w).start()
    for k in range(Y - 1):
        fy(k, w).start()

    weight = weight_ref[...]
    weight_t = weight.astype(f32).T.astype(bf16)
    bias = jnp.broadcast_to(bias_ref[...], (perm_ref.shape[1], bias_ref.shape[1])).T
    classes = cls_ref.shape[1]
    cpad[...] = jnp.zeros_like(cpad)
    cpad[:, :classes] = cls_ref[...]

    nodes = perm_ref.shape[1]
    slots = unpack.shape[0] // wide
    perm_row = jnp.broadcast_to(perm_ref[...], (nodes, nodes))
    perm_col = perm_row.astype(f32).T.astype(jnp.int32)
    dest_row, dest_col = perm_row // nodes, perm_col // nodes
    sub = lax.broadcasted_iota(jnp.int32, (nodes, nodes), 0)
    lane = lax.broadcasted_iota(jnp.int32, (nodes, nodes), 1)
    rank = jnp.sum(((dest_row == dest_col) & (sub < lane)).astype(jnp.int32), axis=0, keepdims=True)
    place_row = perm_ref[...] // nodes * slots + rank
    chosen = (
        lax.broadcasted_iota(jnp.int32, (wide * slots, nodes), 0) == place_row
    ).astype(f32).astype(bf16)
    where_to = (perm_col - dest_col * nodes == lane).astype(f32).astype(bf16)
    hidden = bias_ref.shape[1]
    pack[:, hidden:] = dot(chosen, where_to, (1, 0)).astype(bf16)

    for k in range(Y - 1):
        slot = xl * Y + ring_from(y, k, Y)
        fy(k, slot).wait_recv()
        fx(k, slot).start()
    tile_copy.wait()
    for k in range(Y):
        fx(k, (1 - xl) * Y + ring_from(y, k, Y)).wait_recv()

    def aggregate(b):
        first = col_ref[2 * b]
        second = jnp.where(count_ref[b] > 1, col_ref[2 * b + 1], wide)
        left = jnp.concatenate([ft[first], ft[second]], axis=1)
        right = jnp.concatenate([tiles[2 * b], tiles[2 * b + 1]], axis=1)
        return dot(left, right, (1, 1))

    def s_copy(g, k):
        return rcopy(sbuf.at[g, k], srecv.at[g, k], s_s.at[g, k], s_r.at[g, k], s_dev)

    def x_copy(k):
        return rcopy(xbuf.at[k], xrecv.at[k], x_s.at[k], x_r.at[k], x_dev)

    def z_copy(k):
        return rcopy(zbuf.at[k], zrecv.at[k], z_s.at[k], z_r.at[k], z_dev(k))

    @pl.loop(0, Z)
    def _(k):
        sbuf[0, k] = aggregate(nid(1 - xh, ring_to(z, k, Z), 1 - c)).astype(bf16)
        s_copy(0, k).start()

    @pl.loop(0, Z)
    def _(k):
        part = aggregate(nid(1 - xh, ring_to(z, k, Z), c))
        s_copy(0, k).wait_recv()
        xbuf[k] = (part + srecv[0, k].astype(f32)).astype(bf16)
        x_copy(k).start()

    @pl.loop(0, Z)
    def _(k):
        sbuf[1, k] = aggregate(nid(xh, ring_to(z, k, Z), 1 - c)).astype(bf16)
        s_copy(1, k).start()

    @pl.loop(0, Z)
    def _(k):
        part = aggregate(nid(xh, ring_to(z, k, Z), c))
        s_copy(1, k).wait_recv()
        own[k] = part + srecv[1, k].astype(f32)

    @pl.loop(0, Z - 1)
    def _(k):
        x_copy(k).wait_recv()
        zbuf[k] = (own[k] + xrecv[k].astype(f32)).astype(bf16)
        z_copy(k).start()

    x_copy(Z - 1).wait_recv()
    total = own[Z - 1] + xrecv[Z - 1].astype(f32)
    for k in range(Z - 1):
        z_copy(k).wait_recv()
        total = total + zrecv[k].astype(f32)

    hidden_pre = split_dot(weight_t, total) + bias
    gate_value = jax.nn.sigmoid(hidden_pre)
    activated = (hidden_pre * gate_value).astype(bf16)
    class_id = lax.broadcasted_iota(jnp.int32, (cpad.shape[1], nodes), 0)
    logits = dot(cpad[...].astype(f32).T.astype(bf16), activated, (1, 0))
    logits = jnp.where(class_id < classes, logits, -jnp.inf)
    top_score = jnp.max(logits, axis=0, keepdims=True)
    shifted = jnp.exp(logits - top_score)
    exp_total = jnp.sum(shifted, axis=0, keepdims=True)
    target = class_id == labels_ref[...]
    grad_logits = shifted / exp_total - target.astype(f32)
    grad_act = split_dot(cpad[...], grad_logits)
    grad_pre = (grad_act * gate_value * (1.0 + hidden_pre * (1.0 - gate_value))).astype(bf16)
    gbuf[n] = dot(weight, grad_pre, (1, 0)).astype(bf16)

    def gz(k, slot):
        return rcopy(gbuf.at[slot], gbuf.at[slot], gz_s.at[k], gz_r.at[k], z_dev(k))

    def gx(k, slot):
        return rcopy(gbuf.at[slot], gbuf.at[slot], gx_s.at[k], gx_r.at[k], x_dev)

    def gs(g, k, slot):
        return rcopy(gbuf.at[slot], gbuf.at[slot], gs_s.at[g, k], gs_r.at[g, k], s_dev)

    for k in range(Z - 2, -1, -1):
        gz(k, n).start()

    pack[:, :hidden] = dot(chosen, activated, (1, 1)).astype(bf16)

    def a_copy(d, src, dst):
        return rcopy(
            pack.at[pl.ds(src * slots, slots)], unpack.at[pl.ds(dst * slots, slots)],
            a_s.at[d], a_r.at[d], ((w + d) % wide, n),
        )

    for d in range(1, wide):
        a_copy(d, (w + d) % wide, w).start()
    mine = pl.ds(pl.multiple_of(w * slots, slots), slots)
    unpack[mine, :] = pack[mine, :]
    picked = jnp.sum(jnp.where(target, logits, 0.0), axis=0, keepdims=True)
    loss_ref[...] = top_score + jnp.log(exp_total) - picked

    def spread(b):
        right = jnp.concatenate([tiles[2 * b], tiles[2 * b + 1]], axis=1)
        part = dot(gbuf[b], right, (1, 0))
        for t in range(2):
            run[2 * b + t + 1] = part[:, t * nodes : (t + 1) * nodes] + run[prev_ref[2 * b + t]]

    @pl.loop(0, Z + LAG + 1)
    def _(j):
        @pl.when(j < Z)
        def _():
            k = Z - 1 - j
            slot = nid(xh, ring_from(z, k, Z), c)

            @pl.when(j > 0)
            def _():
                gz(k, slot).wait_recv()

            gx(k, slot).start()
            gs(0, k, slot).start()
            spread(slot)

        @pl.when((j >= LAG) & (j < Z + LAG))
        def _():
            k = Z - 1 - j + LAG
            slot = nid(1 - xh, ring_from(z, k, Z), c)
            gx(k, slot).wait_recv()
            gs(1, k, slot).start()
            spread(slot)

        @pl.when((j >= 1) & (j < Z + 1))
        def _():
            k = Z - j
            slot = nid(xh, ring_from(z, k, Z), 1 - c)
            gs(0, k, slot).wait_recv()
            spread(slot)

        @pl.when(j >= LAG + 1)
        def _():
            k = Z - j + LAG
            slot = nid(1 - xh, ring_from(z, k, Z), 1 - c)
            gs(1, k, slot).wait_recv()
            spread(slot)

    last = narrow * 2

    def cx(k):
        return rcopy(cxbuf.at[k], cxrecv.at[k], cx_s.at[k], cx_r.at[k], xl_dev)

    def cy(k):
        return rcopy(cybuf.at[k], cyrecv.at[k], cy_s.at[k], cy_r.at[k], y_dev(k))

    for k in range(Y):
        cxbuf[k] = run[prev_ref[last + (1 - xl) * Y + ring_to(y, k, Y)]].astype(bf16)
        cx(k).start()

    for d in range(1, wide):
        a_copy(d, w, (w + wide - d) % wide).wait_recv()
    next_ref[...] = dot(unpack[:, hidden:], unpack[:, :hidden], (0, 0)).astype(bf16)

    for k in range(Y):
        part = run[prev_ref[last + xl * Y + ring_to(y, k, Y)]]
        cx(k).wait_recv()
        part = part + cxrecv[k].astype(f32)
        if k < Y - 1:
            cybuf[k] = part.astype(bf16)
            cy(k).start()
    for k in range(Y - 1):
        cy(k).wait_recv()
        part = part + cyrecv[k].astype(f32)
    grad_ref[...] = part.T

    for k in range(Y):
        fx(k, w).wait_send()
        cx(k).wait_send()
        if k < Y - 1:
            fy(k, w).wait_send()
            cy(k).wait_send()
    for d in range(1, wide):
        a_copy(d, (w + d) % wide, w).wait_send()

    @pl.loop(0, Z)
    def _(k):
        s_copy(0, k).wait_send()
        s_copy(1, k).wait_send()
        x_copy(k).wait_send()
        gx(k, n).wait_send()
        gs(0, k, n).wait_send()
        gs(1, k, n).wait_send()

    @pl.loop(0, Z - 1)
    def _(k):
        z_copy(k).wait_send()
        gz(k, n).wait_send()


def chain_table(columns, counts, wide, narrow):
    size = narrow // 4
    n = lax.axis_index("narrow")
    slot = lax.iota(jnp.int32, narrow * 2)
    b = slot // 2
    xb, zb, cb = b // (2 * size), (b // 2) % size, b % 2
    far = ((n // 2) % size - zb + size) % size
    half = size // 2
    k = jnp.where(far > half, 2 * (far - half), jnp.where(far == half, 0, 2 * (half - far) - 1))
    other_x, other_c = xb != n // (2 * size), cb != n % 2
    step = size - 1 - k + jnp.where(other_x, LAG, 0) + jnp.where(other_c, 1, 0)
    kind = jnp.where(other_x, 1, 0) + jnp.where(other_c, 2, 0)
    when = step * 4 + kind
    column = jnp.where(slot % 2 < counts[b], columns, wide)
    key = when * 256 + slot + 1
    ask_column = jnp.concatenate([column, jnp.arange(wide, dtype=jnp.int32)])
    ask_before = jnp.concatenate([when * 256, jnp.full((wide,), 1 << 30, jnp.int32)])
    fits = (column[None, :] == ask_column[:, None]) & (key[None, :] < ask_before[:, None])
    return jnp.max(jnp.where(fits, key[None, :], 0), axis=1) % 256


def per_device(
    wide, narrow, features, in_weight, hidden_bias, classifier, adjacency_tiles, tile_col, tile_count, node_perm, labels
):
    nodes, f_in = features.shape[1], features.shape[2]
    hidden = in_weight.shape[1]
    tile = adjacency_tiles.shape[3]
    Y, Z = wide // 2, narrow // 4
    columns = tile_col.reshape(-1)
    counts = tile_count.reshape(-1)
    table = chain_table(columns, counts, wide, narrow)
    padded = -(-classifier.shape[1] // 128) * 128
    slots = 16
    block = (f_in, tile)
    vmem = pl.BlockSpec(memory_space=pltpu.VMEM)
    smem = pl.BlockSpec(memory_space=pltpu.SMEM)
    dma = pltpu.SemaphoreType.DMA
    next_rows, node_loss, input_grad = pl.pallas_call(
        functools.partial(layer_kernel, wide, narrow),
        out_shape=(
            jax.ShapeDtypeStruct((nodes, hidden), bf16),
            jax.ShapeDtypeStruct((1, nodes), f32),
            jax.ShapeDtypeStruct((nodes, f_in), f32),
        ),
        in_specs=[vmem, vmem, vmem, vmem, pl.BlockSpec(memory_space=pl.ANY), smem, smem, smem, vmem, vmem],
        out_specs=(vmem, vmem, vmem),
        scratch_shapes=[
            pltpu.VMEM((narrow * 2, tile, tile), bf16),
            pltpu.VMEM((wide + 1,) + block, bf16),
            pltpu.VMEM((2, Z) + block, bf16),
            pltpu.VMEM((2, Z) + block, bf16),
            pltpu.VMEM((Z,) + block, bf16),
            pltpu.VMEM((Z,) + block, bf16),
            pltpu.VMEM((Z - 1,) + block, bf16),
            pltpu.VMEM((Z - 1,) + block, bf16),
            pltpu.VMEM((Z,) + block, f32),
            pltpu.VMEM((narrow,) + block, bf16),
            pltpu.VMEM((narrow * 2 + 1,) + block, f32),
            pltpu.VMEM((wide * slots, hidden + nodes), bf16),
            pltpu.VMEM((wide * slots, hidden + nodes), bf16),
            pltpu.VMEM((Y,) + block, bf16),
            pltpu.VMEM((Y,) + block, bf16),
            pltpu.VMEM((Y - 1,) + block, bf16),
            pltpu.VMEM((Y - 1,) + block, bf16),
            pltpu.VMEM((hidden, padded), bf16),
            dma,
            dma((Y - 1,)), dma((Y - 1,)), dma((Y,)), dma((Y,)),
            dma((2, Z)), dma((2, Z)), dma((Z,)), dma((Z,)), dma((Z - 1,)), dma((Z - 1,)),
            dma((Z - 1,)), dma((Z - 1,)), dma((Z,)), dma((Z,)), dma((2, Z)), dma((2, Z)),
            dma((Y,)), dma((Y,)), dma((Y - 1,)), dma((Y - 1,)), dma((wide,)), dma((wide,)),
        ],
        compiler_params=pltpu.CompilerParams(
            collective_id=0, has_side_effects=True, vmem_limit_bytes=48 * 2**20
        ),
        name="layer",
    )(
        features.reshape(nodes, f_in), in_weight, hidden_bias.reshape(1, hidden), classifier,
        adjacency_tiles.reshape(-1, tile, tile), columns, counts, table, node_perm, labels.reshape(1, nodes),
    )
    return next_rows.reshape(1, nodes, hidden), node_loss.reshape(nodes), input_grad.reshape(1, nodes, f_in)


def solution(mesh):
    in_specs = (
        P("narrow", "wide", None),
        P(),
        P(),
        P(),
        P("wide", "narrow", None, None, None),
        P("wide", "narrow", None),
        P("wide", "narrow"),
        P("narrow", "wide"),
        P(("wide", "narrow")),
    )
    out_specs = (P("narrow", "wide", None), P(("wide", "narrow")), P("narrow", "wide", None))
    return jax.shard_map(
        functools.partial(per_device, mesh.shape["wide"], mesh.shape["narrow"]),
        mesh=mesh, in_specs=in_specs, out_specs=out_specs, check_vma=False,
    )
```

time: 518 us -> 105 us (0.20)
  the two profiles are of different devices: /device:TPU:6 before, /device:TPU:1 now
where the time goes in v1:
time: 105 us
  Pallas kernels  92.1 us (88%)
  local copies, waits for them, and re-layouts  11.4 us (11%)
    pallas_call x1, Pallas kernels, per_device(): pl.pallas_call(functools.partial(layer_kernel, wide, narrow), out_shape=(...  92.1 us
    unnamed x19, local copies, waits for them, and re-layouts  9.66 us

profile of v1, /device:TPU:1, one launch (start us, length us, event | category | flops | bytes accessed | tf_op | source)
XLA Modules:
  0.0 104.5 jit_solution(14202993182938478681)
XLA Ops:
  0.7 1.6 %gather_fusion = s32[96]{0:T(128)S(1)} fusion(s32[48]{0:T(128)} %bitcast.12, s32[1024]{0:T(1024)S(1)} %pad_clamp_fusion), kind=kCustom, calls=%fused_computation | custom fusion | bytes 1152 | tf_op jit(solution)/shard_map/gather | solution.py:328
  2.3 0.8 copy.16
  3.1 0.1 reshape.182.col_ref
  3.3 0.1 pad_add_fusion
  3.3 0.1 select_reduce_fusion
  3.5 1.0 copy.17.cls_ref
  4.5 0.0 copy-start
  4.5 0.6 copy-done
  5.1 0.0 copy-start.1
  5.1 1.9 %copy-done.1 = bf16[48,1,2,128,128]{4,3,2,1,0:T(8,128)(2,1)S(1)} copy-done((bf16[48,1,2,128,128]{4,3,2,1,0:T(8,128)(2,1)S(1)}, bf16[48,1,2,128,128]{4,3,2,1,0:T(8,128)(2,1)}, u32[]{:S(2)}) %copy-start.1) | copy-done | bytes 3145752
  7.0 0.0 copy-start.2
  7.0 0.8 copy-done.2
  7.9 0.0 copy-start.3
  7.9 0.8 copy-done.3
  8.6 0.0 copy-start.4
  8.6 0.7 copy-done.4
  9.3 0.0 copy-start.5
  9.3 0.7 copy-done.5
  9.9 0.0 copy-start.6
  9.9 0.7 copy-done.6
  10.6 92.1 %layer.1 = (bf16[128,256]{1,0:T(8,128)(2,1)S(1)}, f32[1,128]{1,0:T(1,128)S(1)}, f32[128,128]{1,0:T(8,128)S(1)}) custom-call(bf16[128,128]{1,0:T(8,128)(2,1)S(1)} %bitcast.17, bf16[128,256]{1,0:T(8,128)(2,1)S(1)} %copy-done.2, f32[1,256]{1,0:T(1,128)S(1)} %bitcast.18, bf16[256,172]{1,0:T(8,128)(2,1)S(1)} %copy.17.cls_ref, bf16[96,128,128]{2,1,0:T(8,128)(2,1)S(1)} %bitcast.14, ...), custom_call_target="tpu_custom_call" | custom-call | tf_op jit(solution)/shard_map/layer/pallas_call | solution.py:352
  102.7 0.6 copy.21
  103.4 0.5 copy.22
  103.9 0.6 copy.23
  (6 shorter events, 0.1 us)
Async XLA Ops:
  4.5 0.7 copy-start
  5.1 1.9 %copy-start.1 = (bf16[48,1,2,128,128]{4,3,2,1,0:T(8,128)(2,1)S(1)}, bf16[48,1,2,128,128]{4,3,2,1,0:T(8,128)(2,1)}, u32[]{:S(2)}) copy-start(bf16[48,1,2,128,128]{4,3,2,1,0:T(8,128)(2,1)} %param.13) | copy-start | bytes 9437188
  7.0 0.8 copy-start.2
  7.9 0.8 copy-start.3
  8.6 0.7 copy-start.4
  9.3 0.7 copy-start.5
  9.9 0.7 copy-start.6

commit v2 on v1

v2 whole, which is shorter than its diff:
```python
import functools

import jax
import jax.numpy as jnp
from jax import lax
from jax.experimental import pallas as pl
from jax.experimental.pallas import tpu as pltpu
from jax.sharding import PartitionSpec as P

MESH = pl.DeviceIdType.MESH
RELAY = 3
INWARD = (6, 5, -5, 4, -4, 3, -3, 2, -2, 1, -1, 0)
FAR, NEAR = INWARD[:5], INWARD[5:]
ARRIVALS = (
    ("own", 0), ("own", 3), ("own", -3), ("own", 1), ("own", -1), ("x", 0), ("own", 2), ("own", -2),
    ("x", 3), ("x", -3), ("x", 1), ("x", -1), ("own", 4), ("own", -4), ("own", 5), ("own", -5), ("own", 6),
    ("x", 2), ("x", -2), ("other", 4), ("other", -4), ("other", 5), ("other", -5), ("other", 6),
)
SIBLING_LAG = 2


def spread_order():
    order = []
    for i in range(len(ARRIVALS) + SIBLING_LAG):
        for j, sibling in ((i, 0), (i - SIBLING_LAG, 1)):
            if 0 <= j < len(ARRIVALS):
                kind, offset = ARRIVALS[j]
                order.append((int(kind != "own"), sibling, offset))
    return order


f32, bf16 = jnp.float32, jnp.bfloat16


def ring_offset(k, size):
    steps = size // 2 - (k + 1) // 2
    return steps * ((k % 2) * 2 - 1)


def ring_step(place, offset, size):
    moved = place + offset
    if offset > 0:
        return jnp.where(moved >= size, moved - size, moved)
    return jnp.where(moved < 0, moved + size, moved) if offset else place


def ring_to(place, k, size):
    return ring_step(place, ring_offset(k, size), size)


def ring_from(place, k, size):
    return ring_step(place, -ring_offset(k, size), size)


def dot(a, b, contract):
    return lax.dot_general(a, b, ((contract[:1], contract[1:]), ((), ())), preferred_element_type=f32)


def split_dot(a, b):
    high = b.astype(bf16)
    low = (b - high.astype(f32)).astype(bf16)
    return dot(a, high, (1, 0)) + dot(a, low, (1, 0))


def turned(row, size):
    return jnp.broadcast_to(row.astype(f32), (size, size)).T.astype(jnp.int32)


def layer_kernel(
    wide, narrow,
    feat_hbm, weight_hbm, bias_hbm, cls_hbm, tiles_hbm, cols_hbm, counts_hbm, perm_hbm, labels_hbm,
    next_ref, loss_ref, grad_ref,
    feat, weight, bias, cls, tiles, cols, counts, perm, labels, table_v, table,
    ft, sbuf, srecv, fbuf, frecv, xbuf, xrecv, zbuf, zrecv, own, gbuf, run,
    pack, unpack, cxbuf, cxrecv, cybuf, cyrecv, cpad,
    in_sem, table_sem, fy_s, fy_r, fx_s, fx_r, s_s, s_r, f_s, f_r, x_s, x_r, z_s, z_r,
    gz_s, gz_r, gx_s, gx_r, gs_s, gs_r, cx_s, cx_r, cy_s, cy_r, a_s, a_r,
):
    Y, Z = wide // 2, narrow // 4
    w, n = lax.axis_index("wide"), lax.axis_index("narrow")
    xl, y = w // Y, w % Y
    xh, z, c = n // (2 * Z), (n // 2) % Z, n % 2

    def nid(xh_, z_, c_):
        return (xh_ * Z + z_) * 2 + c_

    def rcopy(src, dst, ss, rs, dev):
        return pltpu.make_async_remote_copy(
            src_ref=src, dst_ref=dst, send_sem=ss, recv_sem=rs, device_id=dev, device_id_type=MESH
        )

    x_dev = (w, nid(1 - xh, z, c))
    s_dev = (w, nid(xh, z, 1 - c))
    xl_dev = ((1 - xl) * Y + y, n)

    sign = 1 - 2 * c

    def zat(offset, facing=1):
        moved = z + sign * (facing * offset)
        return jnp.where(moved < 0, moved + Z, jnp.where(moved >= Z, moved - Z, moved))

    def z_dev(offset):
        return (w, nid(xh, zat(offset), c))

    def y_dev(k):
        return (xl * Y + ring_to(y, k, Y), n)

    def w_dev(d):
        return (ring_step(w, d, wide), n)

    barrier = pltpu.get_barrier_semaphore()
    partners = [w_dev(d) for d in range(1, wide)] + [z_dev(o) for o in (1, -1, 2, -2, 3, -3)] + [x_dev, s_dev]
    for partner in partners:
        pl.semaphore_signal(barrier, inc=1, device_id=partner, device_id_type=MESH)

    inputs = [
        pltpu.make_async_copy(src, dst, in_sem.at[i])
        for i, (src, dst) in enumerate((
            (feat_hbm, feat), (cols_hbm, cols), (counts_hbm, counts), (perm_hbm, perm), (weight_hbm, weight),
            (bias_hbm, bias), (cls_hbm, cls), (labels_hbm, labels), (tiles_hbm, tiles),
        ))
    ]
    for copy in inputs:
        copy.start()
    run[0] = jnp.zeros_like(run[0])
    ft[wide] = jnp.zeros_like(ft[wide])
    table_v[...] = jnp.full(table_v.shape, -1, jnp.int32)
    cpad[...] = jnp.zeros_like(cpad)
    inputs[0].wait()
    ft[w] = feat[...].astype(f32).T.astype(bf16)

    for copy in inputs[1:4]:
        copy.wait()
    nodes = perm.shape[1]
    table_v[0:2, :narrow] = cols[...]
    table_v[2:3, :narrow] = counts[...]
    lane_row = lax.broadcasted_iota(jnp.int32, (1, nodes), 1)
    in_upper = (lane_row >= 2 * Z).astype(jnp.int32)
    in_half = lane_row - 2 * Z * in_upper
    far = ((in_half >> 1) - z) * (1 - 2 * (in_half & 1))
    far = jnp.where(far < 0, far + Z, far)
    other_x, other_c = jnp.abs(in_upper - xh), jnp.abs((in_half & 1) - c)
    kind = (other_x * 2 + other_c) * Z + far
    when = jnp.zeros_like(far)
    for turn, (column_, core, offset) in enumerate(spread_order()):
        when = jnp.where(kind == (column_ * 2 + core) * Z + offset % Z, turn, when)
    column = [table_v[0:1, :], jnp.where(table_v[2:3, :] > 1, table_v[1:2, :], jnp.where(lane_row < narrow, wide, -1))]
    key = [when * 256 + 2 * lane_row + 1 + t for t in range(2)]
    column_down = [turned(row, nodes) for row in column]
    key_down = [turned(row, nodes) for row in key]
    for t in range(2):
        fits = [
            jnp.where((column_down[u] == column[t]) & (key_down[u] < when * 256), key_down[u], 0) for u in range(2)
        ]
        table_v[2 + t : 3 + t, :] = jnp.max(jnp.maximum(fits[0], fits[1]), axis=0, keepdims=True) & 255
    fits = [jnp.where(column_down[u] == lane_row, key_down[u], 0) for u in range(2)]
    table_v[4:5, :] = jnp.max(jnp.maximum(fits[0], fits[1]), axis=0, keepdims=True) & 255
    table_v[1:2, :] = column[1]
    table_copy = pltpu.make_async_copy(table_v, table, table_sem)
    table_copy.start()

    pl.semaphore_wait(barrier, len(partners))

    def fy(k, slot):
        return rcopy(ft.at[slot], ft.at[slot], fy_s.at[k], fy_r.at[k], y_dev(k))

    def fx(k, slot):
        return rcopy(ft.at[slot], ft.at[slot], fx_s.at[k], fx_r.at[k], xl_dev)

    fx(Y - 1, w).start()
    for k in range(Y - 1):
        fy(k, w).start()

    slots = unpack.shape[0] // wide
    hidden = bias.shape[1]
    perm_row = perm[...]
    shift = nodes.bit_length() - 1
    dest_row, perm_col = perm_row >> shift, turned(perm_row, nodes)
    dest_col = perm_col >> shift
    sub = lax.broadcasted_iota(jnp.int32, (nodes, nodes), 0)
    lane = lax.broadcasted_iota(jnp.int32, (nodes, nodes), 1)
    rank = jnp.sum(((dest_row == dest_col) & (sub < lane)).astype(jnp.int32), axis=0, keepdims=True)
    place_row = dest_row * slots + rank
    chosen = (
        lax.broadcasted_iota(jnp.int32, (wide * slots, nodes), 0) == place_row
    ).astype(f32).astype(bf16)
    where_to = (perm_col - dest_col * nodes == lane).astype(f32).astype(bf16)
    pack[:, hidden:] = dot(chosen, where_to, (1, 0)).astype(bf16)

    for copy in inputs[4:8]:
        copy.wait()
    weight_t = weight[...].astype(f32).T.astype(bf16)
    bias_t = jnp.broadcast_to(bias[...], (nodes, hidden)).T
    classes = cls.shape[0]
    cpad[:classes, :] = cls[...]
    cls_t = cpad[...].astype(f32).T.astype(bf16)

    for k in range(Y - 1):
        slot = xl * Y + ring_from(y, k, Y)
        fy(k, slot).wait_recv()
        fx(k, slot).start()
    table_copy.wait()
    inputs[8].wait()
    for k in range(Y):
        fx(k, (1 - xl) * Y + ring_from(y, k, Y)).wait_recv()

    def aggregate(b):
        left = jnp.concatenate([ft[table[0, b]], ft[table[1, b]]], axis=1)
        right = jnp.concatenate([tiles[2 * b], tiles[2 * b + 1]], axis=1)
        return dot(left, right, (1, 1))

    def s_copy(g, k):
        return rcopy(sbuf.at[g, k], srecv.at[g, k], s_s.at[g, k], s_r.at[g, k], s_dev)

    def x_copy(k):
        return rcopy(xbuf.at[k], xrecv.at[k], x_s.at[k], x_r.at[k], x_dev)

    def far_copy(g, k):
        relay = FAR[k] - RELAY if FAR[k] > 0 else FAR[k] + RELAY
        return rcopy(fbuf.at[g, k], frecv.at[g, k], f_s.at[g, k], f_r.at[g, k], z_dev(relay))

    def z_copy(k):
        return rcopy(zbuf.at[k], zrecv.at[k], z_s.at[k], z_r.at[k], z_dev(NEAR[k]))

    columns = (1 - xh, xh)

    def begin(g, k):
        sbuf[g, k] = aggregate(nid(columns[g], zat(INWARD[k], -1), 1 - c)).astype(bf16)
        s_copy(g, k).start()
        own[g, k] = aggregate(nid(columns[g], zat(INWARD[k]), c))

    def chip_sum(g, k):
        s_copy(g, k).wait_recv()
        return own[g, k] + srecv[g, k].astype(f32)

    def add_far(g, k, part):
        for u in range(5):
            if FAR[u] * NEAR[k] > 0:
                far_copy(g, u).wait_recv()
                part = part + frecv[g, u].astype(f32)
        return part

    for g in range(2):
        for k in range(5):
            begin(g, k)
    for k in range(5, Z):
        begin(0, k)
        if k < 10:
            fbuf[0, k - 5] = chip_sum(0, k - 5).astype(bf16)
            far_copy(0, k - 5).start()
    for k in range(5, Z):
        begin(1, k)
        if k < 10:
            fbuf[1, k - 5] = chip_sum(1, k - 5).astype(bf16)
            far_copy(1, k - 5).start()
    for k in range(2, 7):
        xbuf[k] = chip_sum(0, k + 5).astype(bf16)
        x_copy(k).start()
    for k in range(2):
        xbuf[k] = add_far(0, k, chip_sum(0, k + 5)).astype(bf16)
        x_copy(k).start()
    for k in range(2, 6):
        part = chip_sum(1, k + 5)
        x_copy(k).wait_recv()
        zbuf[k] = (part + xrecv[k].astype(f32)).astype(bf16)
        z_copy(k).start()
    for k in range(2):
        part = add_far(1, k, chip_sum(1, k + 5))
        x_copy(k).wait_recv()
        zbuf[k] = (part + xrecv[k].astype(f32)).astype(bf16)
        z_copy(k).start()
    total = chip_sum(1, Z - 1)
    x_copy(6).wait_recv()
    total = total + xrecv[6].astype(f32)
    for k in (2, 3, 4, 5, 0, 1):
        z_copy(k).wait_recv()
        total = total + zrecv[k].astype(f32)

    def wait_forward():
        for k in range(Y):
            fx(k, w).wait_send()
            if k < Y - 1:
                fy(k, w).wait_send()
        for k in range(Z):
            s_copy(0, k).wait_send()
            s_copy(1, k).wait_send()
        for k in range(5):
            far_copy(0, k).wait_send()
            far_copy(1, k).wait_send()
        for k in range(7):
            x_copy(k).wait_send()
        for k in range(6):
            z_copy(k).wait_send()


    hidden_pre = split_dot(weight_t, total) + bias_t
    gate_value = jax.nn.sigmoid(hidden_pre)
    activated = (hidden_pre * gate_value).astype(bf16)
    class_id = lax.broadcasted_iota(jnp.int32, (cpad.shape[0], nodes), 0)
    logits = dot(cpad[...], activated, (1, 0))
    logits = jnp.where(class_id < classes, logits, -jnp.inf)
    top_score = jnp.max(logits, axis=0, keepdims=True)
    shifted = jnp.exp(logits - top_score)
    exp_total = jnp.sum(shifted, axis=0, keepdims=True)
    target = class_id == labels[...]
    grad_logits = shifted / exp_total - target.astype(f32)
    grad_act = split_dot(cls_t, grad_logits)
    grad_pre = (grad_act * gate_value * (1.0 + hidden_pre * (1.0 - gate_value))).astype(bf16)
    gbuf[n] = dot(weight[...], grad_pre, (1, 0)).astype(bf16)

    def gz(g, offset, slot, towards):
        k = INWARD.index(offset)
        return rcopy(gbuf.at[slot], gbuf.at[slot], gz_s.at[g, k], gz_r.at[g, k], z_dev(towards))

    def gx(offset, slot):
        k = INWARD.index(offset)
        return rcopy(gbuf.at[slot], gbuf.at[slot], gx_s.at[k], gx_r.at[k], x_dev)

    def gs(g, offset, slot):
        k = INWARD.index(offset)
        return rcopy(gbuf.at[slot], gbuf.at[slot], gs_s.at[g, k], gs_r.at[g, k], s_dev)

    def pass_on(g, offset, slot):
        if offset == -RELAY:
            for further, seen_at in ((3, 6), (2, -5), (1, -4)):
                gz(g, seen_at, slot, further).start()
        if offset == RELAY:
            for further, seen_at in ((-2, 5), (-1, 4)):
                gz(g, seen_at, slot, further).start()

    gx(0, n).start()
    for offset in (3, -3, 1, -1, 2, -2):
        gz(0, -offset, n, offset).start()
    gs(0, 0, n).start()

    pack[:, :hidden] = dot(chosen, activated, (1, 1)).astype(bf16)

    def a_copy(d, src, dst):
        return rcopy(
            pack.at[pl.ds(src * slots, slots)], unpack.at[pl.ds(dst * slots, slots)],
            a_s.at[d], a_r.at[d], w_dev(d),
        )

    for d in range(1, wide):
        a_copy(d, ring_step(w, d, wide), w).start()
    mine = pl.ds(pl.multiple_of(w * slots, slots), slots)
    unpack[mine, :] = pack[mine, :]
    picked = jnp.sum(jnp.where(target, logits, 0.0), axis=0, keepdims=True)
    loss_ref[...] = top_score + jnp.log(exp_total) - picked

    def spread(b):
        right = jnp.concatenate([tiles[2 * b], tiles[2 * b + 1]], axis=1)
        part = dot(gbuf[b], right, (1, 0))
        for t in range(2):
            run[2 * b + t + 1] = part[:, t * nodes : (t + 1) * nodes] + run[table[2 + t, b]]

    for i in range(len(ARRIVALS) + SIBLING_LAG):
        ready = []
        if i < len(ARRIVALS):
            kind, offset = ARRIVALS[i]
            g = int(kind != "own")
            slot = nid(xh if g == 0 else 1 - xh, zat(offset), c)
            if kind == "x":
                gx(offset, slot).wait_recv()
                pass_on(1, offset, slot)
                gs(1, offset, slot).start()
            elif offset:
                gz(g, offset, slot, 1).wait_recv()
                if kind == "own":
                    pass_on(0, offset, slot)
                    if offset in NEAR:
                        gx(offset, slot).start()
                gs(g, offset, slot).start()
            ready.append(slot)
        if i >= SIBLING_LAG:
            kind, offset = ARRIVALS[i - SIBLING_LAG]
            g = int(kind != "own")
            slot = nid(xh if g == 0 else 1 - xh, zat(offset, -1), 1 - c)
            gs(g, offset, slot).wait_recv()
            ready.append(slot)
        for slot in ready:
            spread(slot)

    def wait_backward():
        for d in range(1, wide):
            a_copy(d, ring_step(w, d, wide), w).wait_send()
        for offset in INWARD:
            gs(0, offset, n).wait_send()
            gs(1, offset, n).wait_send()
            if offset in NEAR:
                gx(offset, n).wait_send()
            else:
                gz(1, offset, n, 1).wait_send()
            if offset:
                gz(0, offset, n, 1).wait_send()

    def place():
        for d in range(1, wide):
            a_copy(d, w, ring_step(w, -d, wide)).wait_recv()
        next_ref[...] = dot(unpack[:, hidden:], unpack[:, :hidden], (0, 0)).astype(bf16)


    def cx(k):
        return rcopy(cxbuf.at[k], cxrecv.at[k], cx_s.at[k], cx_r.at[k], xl_dev)

    def cy(k):
        return rcopy(cybuf.at[k], cyrecv.at[k], cy_s.at[k], cy_r.at[k], y_dev(k))

    for k in range(Y):
        cxbuf[k] = run[table[4, (1 - xl) * Y + ring_to(y, k, Y)]].astype(bf16)
        cx(k).start()

    place()

    for k in range(Y):
        part = run[table[4, xl * Y + ring_to(y, k, Y)]]
        cx(k).wait_recv()
        part = part + cxrecv[k].astype(f32)
        if k < Y - 1:
            cybuf[k] = part.astype(bf16)
            cy(k).start()
    for k in range(Y - 1):
        cy(k).wait_recv()
        part = part + cyrecv[k].astype(f32)
    grad_ref[...] = part.T

    wait_forward()
    wait_backward()
    for k in range(Y):
        cx(k).wait_send()
        if k < Y - 1:
            cy(k).wait_send()


def per_device(
    wide, narrow, features, in_weight, hidden_bias, classifier, adjacency_tiles, tile_col, tile_count, node_perm, labels
):
    nodes, f_in = features.shape[1], features.shape[2]
    hidden = in_weight.shape[1]
    tile = adjacency_tiles.shape[3]
    Y, Z = wide // 2, narrow // 4
    padded = -(-classifier.shape[1] // 128) * 128
    slots = 16
    block = (f_in, tile)
    vmem = pl.BlockSpec(memory_space=pltpu.VMEM)
    hbm = pl.BlockSpec(memory_space=pltpu.HBM)
    dma = pltpu.SemaphoreType.DMA
    next_rows, node_loss, input_grad = pl.pallas_call(
        functools.partial(layer_kernel, wide, narrow),
        out_shape=(
            pltpu.VMEM((nodes, hidden), bf16),
            pltpu.VMEM((1, nodes), f32),
            pltpu.VMEM((nodes, f_in), f32),
        ),
        in_specs=[hbm] * 9,
        out_specs=(vmem, vmem, vmem),
        scratch_shapes=[
            pltpu.VMEM((nodes, f_in), bf16),
            pltpu.VMEM((f_in, hidden), bf16),
            pltpu.VMEM((1, hidden), f32),
            pltpu.VMEM(classifier.shape[::-1], bf16),
            pltpu.VMEM((narrow * 2, tile, tile), bf16),
            pltpu.VMEM((2, narrow), jnp.int32),
            pltpu.VMEM((1, narrow), jnp.int32),
            pltpu.VMEM((1, nodes), jnp.int32),
            pltpu.VMEM((1, nodes), jnp.int32),
            pltpu.VMEM((8, nodes), jnp.int32),
            pltpu.SMEM((8, nodes), jnp.int32),
            pltpu.VMEM((wide + 1,) + block, bf16),
            pltpu.VMEM((2, Z) + block, bf16),
            pltpu.VMEM((2, Z) + block, bf16),
            pltpu.VMEM((2, 5) + block, bf16),
            pltpu.VMEM((2, 5) + block, bf16),
            pltpu.VMEM((7,) + block, bf16),
            pltpu.VMEM((7,) + block, bf16),
            pltpu.VMEM((6,) + block, bf16),
            pltpu.VMEM((6,) + block, bf16),
            pltpu.VMEM((2, Z) + block, f32),
            pltpu.VMEM((narrow,) + block, bf16),
            pltpu.VMEM((narrow * 2 + 1,) + block, f32),
            pltpu.VMEM((wide * slots, hidden + nodes), bf16),
            pltpu.VMEM((wide * slots, hidden + nodes), bf16),
            pltpu.VMEM((Y,) + block, bf16),
            pltpu.VMEM((Y,) + block, bf16),
            pltpu.VMEM((Y - 1,) + block, bf16),
            pltpu.VMEM((Y - 1,) + block, bf16),
            pltpu.VMEM((padded, hidden), bf16),
            dma((9,)), dma,
            dma((Y - 1,)), dma((Y - 1,)), dma((Y,)), dma((Y,)),
            dma((2, Z)), dma((2, Z)), dma((2, 5)), dma((2, 5)), dma((7,)), dma((7,)), dma((6,)), dma((6,)),
            dma((2, Z)), dma((2, Z)), dma((Z,)), dma((Z,)), dma((2, Z)), dma((2, Z)),
            dma((Y,)), dma((Y,)), dma((Y - 1,)), dma((Y - 1,)), dma((wide,)), dma((wide,)),
        ],
        compiler_params=pltpu.CompilerParams(
            collective_id=0, has_side_effects=True, vmem_limit_bytes=61 * 2**20
        ),
        name="layer",
    )(
        features.reshape(nodes, f_in), in_weight, hidden_bias.reshape(1, hidden), classifier.T,
        adjacency_tiles.reshape(-1, tile, tile), tile_col.transpose(1, 2, 0).reshape(-1, narrow),
        tile_count.reshape(1, narrow), node_perm, labels.reshape(1, nodes),
    )
    return next_rows.reshape(1, nodes, hidden), node_loss.reshape(nodes), input_grad.reshape(1, nodes, f_in)


def solution(mesh):
    in_specs = (
        P("narrow", "wide", None),
        P(),
        P(),
        P(),
        P("wide", "narrow", None, None, None),
        P("wide", "narrow", None),
        P("wide", "narrow"),
        P("narrow", "wide"),
        P(("wide", "narrow")),
    )
    out_specs = (P("narrow", "wide", None), P(("wide", "narrow")), P("narrow", "wide", None))
    return jax.shard_map(
        functools.partial(per_device, mesh.shape["wide"], mesh.shape["narrow"]),
        mesh=mesh, in_specs=in_specs, out_specs=out_specs, check_vma=False,
    )
```

time: 105 us -> 82.1 us (0.78)
  Pallas kernels: 92.1 us -> 79.1 us
  local copies, waits for them, and re-layouts: 11.4 us -> 1.77 us
    pallas_call x1, Pallas kernels: 92.1 us -> 79.1 us  [per_device(): pl.pallas_call(functools.partial(layer_kernel, wide, narrow), out_shape=(...]
    unnamed x19 -> x3, local copies, waits for them, and re-layouts: 9.66 us -> 1.77 us
    gather x1 -> x0, local copies, waits for them, and re-layouts: 1.59 us -> none  [chain_table(): column = jnp.where(slot % 2 < counts[b], columns, wide)]
where the time goes in v2:
time: 82.1 us; the launch traced here: 81.5 us
  Pallas kernels  79.1 us (96%)
  local copies, waits for them, and re-layouts  1.77 us (2%)
    pallas_call x1, Pallas kernels, per_device(): pl.pallas_call(functools.partial(layer_kernel, wide, narrow), out_shape=(...  79.1 us
    unnamed x3, local copies, waits for them, and re-layouts  1.77 us

profile of v2, /device:TPU:1, one launch (start us, length us, event | category | flops | bytes accessed | tf_op | source)
XLA Modules:
  0.0 81.5 jit_solution(1412288113773959287)
XLA Ops:
  0.6 79.1 %layer.1 = (bf16[128,256]{1,0:T(8,128)(2,1)S(1)}, f32[1,128]{1,0:T(1,128)S(1)}, f32[128,128]{1,0:T(8,128)S(1)}) custom-call(bf16[128,128]{1,0:T(8,128)(2,1)} %bitcast.17, bf16[128,256]{1,0:T(8,128)(2,1)} %weight_hbm.1, f32[1,256]{1,0:T(1,128)} %bitcast.18, bf16[172,256]{1,0:T(8,128)(2,1)} %bitcast.16, bf16[96,128,128]{2,1,0:T(8,128)(2,1)} %bitcast.15, ...), custom_call_target="tpu_custom_call" | custom-call | tf_op jit(solution)/shard_map/layer/pallas_call | solution.py:448
  79.7 0.6 copy.15
  80.4 0.5 copy.16
  80.9 0.6 copy.17

commit v3 on v2

--- a/solution.py
+++ b/solution.py
@@ -11,12 +11,13 @@
 RELAY = 3
 INWARD = (6, 5, -5, 4, -4, 3, -3, 2, -2, 1, -1, 0)
 FAR, NEAR = INWARD[:5], INWARD[5:]
+Y_FAR, Y_NEAR = (4, 3, -3), (2, -2, 1, -1)
 ARRIVALS = (
     ("own", 0), ("own", 3), ("own", -3), ("own", 1), ("own", -1), ("x", 0), ("own", 2), ("own", -2),
     ("x", 3), ("x", -3), ("x", 1), ("x", -1), ("own", 4), ("own", -4), ("own", 5), ("own", -5), ("own", 6),
     ("x", 2), ("x", -2), ("other", 4), ("other", -4), ("other", 5), ("other", -5), ("other", 6),
 )
-SIBLING_LAG = 2
+SIBLING_LAG = 6
 
 
 def spread_order():
@@ -72,9 +73,9 @@
     next_ref, loss_ref, grad_ref,
     feat, weight, bias, cls, tiles, cols, counts, perm, labels, table_v, table,
     ft, sbuf, srecv, fbuf, frecv, xbuf, xrecv, zbuf, zrecv, own, gbuf, run,
-    pack, unpack, cxbuf, cxrecv, cybuf, cyrecv, cpad,
+    pack, unpack, cxbuf, cxrecv, cybuf, cyrecv, cnbuf, cnrecv, cpad,
     in_sem, table_sem, fy_s, fy_r, fx_s, fx_r, s_s, s_r, f_s, f_r, x_s, x_r, z_s, z_r,
-    gz_s, gz_r, gx_s, gx_r, gs_s, gs_r, cx_s, cx_r, cy_s, cy_r, a_s, a_r,
+    gz_s, gz_r, gx_s, gx_r, gs_s, gs_r, cx_s, cx_r, cy_s, cy_r, cn_s, cn_r, a_s, a_r,
 ):
     Y, Z = wide // 2, narrow // 4
     w, n = lax.axis_index("wide"), lax.axis_index("narrow")
@@ -209,11 +210,14 @@
         right = jnp.concatenate([tiles[2 * b], tiles[2 * b + 1]], axis=1)
         return dot(left, right, (1, 1))
 
-    def s_copy(g, k):
-        return rcopy(sbuf.at[g, k], srecv.at[g, k], s_s.at[g, k], s_r.at[g, k], s_dev)
-
-    def x_copy(k):
-        return rcopy(xbuf.at[k], xrecv.at[k], x_s.at[k], x_r.at[k], x_dev)
+    parts = (pl.ds(0, 5), pl.ds(5, Z - 5))
+
+    def s_copy(g, p):
+        return rcopy(sbuf.at[g, parts[p]], srecv.at[g, parts[p]], s_s.at[g, p], s_r.at[g, p], s_dev)
+
+    def x_copy(p):
+        span = (pl.ds(0, 2), pl.ds(2, 5))[p]
+        return rcopy(xbuf.at[span], xrecv.at[span], x_s.at[p], x_r.at[p], x_dev)
 
     def far_copy(g, k):
         relay = FAR[k] - RELAY if FAR[k] > 0 else FAR[k] + RELAY
@@ -223,14 +227,18 @@
         return rcopy(zbuf.at[k], zrecv.at[k], z_s.at[k], z_r.at[k], z_dev(NEAR[k]))
 
     columns = (1 - xh, xh)
-
-    def begin(g, k):
-        sbuf[g, k] = aggregate(nid(columns[g], zat(INWARD[k], -1), 1 - c)).astype(bf16)
-        s_copy(g, k).start()
-        own[g, k] = aggregate(nid(columns[g], zat(INWARD[k]), c))
+    spans = (range(5), range(5, Z))
+
+    def for_sibling(g, p):
+        for k in spans[p]:
+            sbuf[g, k] = aggregate(nid(columns[g], zat(INWARD[k], -1), 1 - c)).astype(bf16)
+        s_copy(g, p).start()
+
+    def for_own(g, p):
+        for k in spans[p]:
+            own[g, k] = aggregate(nid(columns[g], zat(INWARD[k]), c))
 
     def chip_sum(g, k):
-        s_copy(g, k).wait_recv()
         return own[g, k] + srecv[g, k].astype(f32)
 
     def add_far(g, k, part):
@@ -240,38 +248,34 @@
                 part = part + frecv[g, u].astype(f32)
         return part
 
+    for p in range(2):
+        for g in range(2):
+            for_sibling(g, p)
+        for g in range(2):
+            for_own(g, p)
     for g in range(2):
+        s_copy(g, 0).wait_recv()
         for k in range(5):
-            begin(g, k)
-    for k in range(5, Z):
-        begin(0, k)
-        if k < 10:
-            fbuf[0, k - 5] = chip_sum(0, k - 5).astype(bf16)
-            far_copy(0, k - 5).start()
-    for k in range(5, Z):
-        begin(1, k)
-        if k < 10:
-            fbuf[1, k - 5] = chip_sum(1, k - 5).astype(bf16)
-            far_copy(1, k - 5).start()
+            fbuf[g, k] = chip_sum(g, k).astype(bf16)
+            far_copy(g, k).start()
+    s_copy(0, 1).wait_recv()
+    s_copy(1, 1).wait_recv()
     for k in range(2, 7):
         xbuf[k] = chip_sum(0, k + 5).astype(bf16)
-        x_copy(k).start()
+    x_copy(1).start()
     for k in range(2):
         xbuf[k] = add_far(0, k, chip_sum(0, k + 5)).astype(bf16)
-        x_copy(k).start()
+    x_copy(0).start()
+    x_copy(1).wait_recv()
     for k in range(2, 6):
-        part = chip_sum(1, k + 5)
-        x_copy(k).wait_recv()
-        zbuf[k] = (part + xrecv[k].astype(f32)).astype(bf16)
+        zbuf[k] = (chip_sum(1, k + 5) + xrecv[k].astype(f32)).astype(bf16)
         z_copy(k).start()
+    sums = [add_far(1, k, chip_sum(1, k + 5)) for k in range(2)]
+    x_copy(0).wait_recv()
     for k in range(2):
-        part = add_far(1, k, chip_sum(1, k + 5))
-        x_copy(k).wait_recv()
-        zbuf[k] = (part + xrecv[k].astype(f32)).astype(bf16)
+        zbuf[k] = (sums[k] + xrecv[k].astype(f32)).astype(bf16)
         z_copy(k).start()
-    total = chip_sum(1, Z - 1)
-    x_copy(6).wait_recv()
-    total = total + xrecv[6].astype(f32)
+    total = chip_sum(1, Z - 1) + xrecv[6].astype(f32)
     for k in (2, 3, 4, 5, 0, 1):
         z_copy(k).wait_recv()
         total = total + zrecv[k].astype(f32)
@@ -281,14 +285,13 @@
             fx(k, w).wait_send()
             if k < Y - 1:
                 fy(k, w).wait_send()
-        for k in range(Z):
-            s_copy(0, k).wait_send()
-            s_copy(1, k).wait_send()
+        for p in range(2):
+            s_copy(0, p).wait_send()
+            s_copy(1, p).wait_send()
+            x_copy(p).wait_send()
         for k in range(5):
             far_copy(0, k).wait_send()
             far_copy(1, k).wait_send()
-        for k in range(7):
-            x_copy(k).wait_send()
         for k in range(6):
             z_copy(k).wait_send()
 
@@ -348,14 +351,16 @@
     picked = jnp.sum(jnp.where(target, logits, 0.0), axis=0, keepdims=True)
     loss_ref[...] = top_score + jnp.log(exp_total) - picked
 
+    wait_forward()
+
     def spread(b):
         right = jnp.concatenate([tiles[2 * b], tiles[2 * b + 1]], axis=1)
         part = dot(gbuf[b], right, (1, 0))
         for t in range(2):
             run[2 * b + t + 1] = part[:, t * nodes : (t + 1) * nodes] + run[table[2 + t, b]]
 
+    ready = []
     for i in range(len(ARRIVALS) + SIBLING_LAG):
-        ready = []
         if i < len(ARRIVALS):
             kind, offset = ARRIVALS[i]
             g = int(kind != "own")
@@ -378,8 +383,10 @@
             slot = nid(xh if g == 0 else 1 - xh, zat(offset, -1), 1 - c)
             gs(g, offset, slot).wait_recv()
             ready.append(slot)
-        for slot in ready:
-            spread(slot)
+        if i % 4 == 3 or i == len(ARRIVALS) + SIBLING_LAG - 1:
+            for slot in ready:
+                spread(slot)
+            ready = []
 
     def wait_backward():
         for d in range(1, wide):
@@ -404,32 +411,64 @@
         return rcopy(cxbuf.at[k], cxrecv.at[k], cx_s.at[k], cx_r.at[k], xl_dev)
 
     def cy(k):
-        return rcopy(cybuf.at[k], cyrecv.at[k], cy_s.at[k], cy_r.at[k], y_dev(k))
-
-    for k in range(Y):
-        cxbuf[k] = run[table[4, (1 - xl) * Y + ring_to(y, k, Y)]].astype(bf16)
+        return rcopy(cybuf.at[k], cyrecv.at[k], cy_s.at[k], cy_r.at[k], (xl * Y + ring_step(y, Y_FAR[k], Y), n))
+
+    def cn(g, k):
+        return rcopy(
+            cnbuf.at[g, k], cnrecv.at[g, k], cn_s.at[g, k], cn_r.at[g, k], (xl * Y + ring_step(y, Y_NEAR[k], Y), n)
+        )
+
+    def column_sum(g, offset):
+        return run[table[4, (xl if g else 1 - xl) * Y + ring_step(y, offset, Y)]]
+
+    for k in range(3):
+        cxbuf[k] = column_sum(0, Y_FAR[k]).astype(bf16)
         cx(k).start()
+    for g in range(2):
+        for k in range(4):
+            cnbuf[g, k] = column_sum(g, Y_NEAR[k]).astype(bf16)
+            cn(g, k).start()
+    for k in range(3):
+        part = column_sum(1, Y_FAR[k])
+        cx(k).wait_recv()
+        cybuf[k] = (part + cxrecv[k].astype(f32)).astype(bf16)
+        cy(k).start()
+    part = column_sum(0, 0)
+    for k in range(4):
+        cn(0, k).wait_recv()
+        part = part + cnrecv[0, k].astype(f32)
+    cxbuf[3] = part.astype(bf16)
+    cx(3).start()
 
     place()
-
-    for k in range(Y):
-        part = run[table[4, xl * Y + ring_to(y, k, Y)]]
-        cx(k).wait_recv()
-        part = part + cxrecv[k].astype(f32)
-        if k < Y - 1:
-            cybuf[k] = part.astype(bf16)
-            cy(k).start()
-    for k in range(Y - 1):
+    wait_backward()
+
+    part = column_sum(1, 0)
+    for k in range(4):
+        cn(1, k).wait_recv()
+        part = part + cnrecv[1, k].astype(f32)
+    for k in range(3):
         cy(k).wait_recv()
         part = part + cyrecv[k].astype(f32)
+    cx(3).wait_recv()
+    part = part + cxrecv[3].astype(f32)
     grad_ref[...] = part.T
 
-    wait_forward()
-    wait_backward()
-    for k in range(Y):
+    for k in range(4):
         cx(k).wait_send()
-        if k < Y - 1:
+        cn(0, k).wait_send()
+        cn(1, k).wait_send()
+        if k < 3:
             cy(k).wait_send()
+
+
+def deliver_kernel(*refs):
+    sems = refs[-1]
+    copies = [pltpu.make_async_copy(refs[i], refs[i + 3], sems.at[i]) for i in range(3)]
+    for copy in copies:
+        copy.start()
+    for copy in copies:
+        copy.wait()
 
 
 def per_device(
@@ -445,7 +484,7 @@
     vmem = pl.BlockSpec(memory_space=pltpu.VMEM)
     hbm = pl.BlockSpec(memory_space=pltpu.HBM)
     dma = pltpu.SemaphoreType.DMA
-    next_rows, node_loss, input_grad = pl.pallas_call(
+    results = pl.pallas_call(
         functools.partial(layer_kernel, wide, narrow),
         out_shape=(
             pltpu.VMEM((nodes, hidden), bf16),
@@ -480,16 +519,18 @@
             pltpu.VMEM((narrow * 2 + 1,) + block, f32),
             pltpu.VMEM((wide * slots, hidden + nodes), bf16),
             pltpu.VMEM((wide * slots, hidden + nodes), bf16),
-            pltpu.VMEM((Y,) + block, bf16),
-            pltpu.VMEM((Y,) + block, bf16),
-            pltpu.VMEM((Y - 1,) + block, bf16),
-            pltpu.VMEM((Y - 1,) + block, bf16),
+            pltpu.VMEM((4,) + block, bf16),
+            pltpu.VMEM((4,) + block, bf16),
+            pltpu.VMEM((3,) + block, bf16),
+            pltpu.VMEM((3,) + block, bf16),
+            pltpu.VMEM((2, 4) + block, bf16),
+            pltpu.VMEM((2, 4) + block, bf16),
             pltpu.VMEM((padded, hidden), bf16),
             dma((9,)), dma,
             dma((Y - 1,)), dma((Y - 1,)), dma((Y,)), dma((Y,)),
-            dma((2, Z)), dma((2, Z)), dma((2, 5)), dma((2, 5)), dma((7,)), dma((7,)), dma((6,)), dma((6,)),
+            dma((2, 2)), dma((2, 2)), dma((2, 5)), dma((2, 5)), dma((2,)), dma((2,)), dma((6,)), dma((6,)),
             dma((2, Z)), dma((2, Z)), dma((Z,)), dma((Z,)), dma((2, Z)), dma((2, Z)),
-            dma((Y,)), dma((Y,)), dma((Y - 1,)), dma((Y - 1,)), dma((wide,)), dma((wide,)),
+            dma((4,)), dma((4,)), dma((3,)), dma((3,)), dma((2, 4)), dma((2, 4)), dma((wide,)), dma((wide,)),
         ],
         compiler_params=pltpu.CompilerParams(
             collective_id=0, has_side_effects=True, vmem_limit_bytes=61 * 2**20
@@ -500,6 +541,15 @@
         adjacency_tiles.reshape(-1, tile, tile), tile_col.transpose(1, 2, 0).reshape(-1, narrow),
         tile_count.reshape(1, narrow), node_perm, labels.reshape(1, nodes),
     )
+    next_rows, node_loss, input_grad = pl.pallas_call(
+        deliver_kernel,
+        out_shape=[jax.ShapeDtypeStruct(result.shape, result.dtype) for result in results],
+        in_specs=[vmem] * 3,
+        out_specs=[hbm] * 3,
+        scratch_shapes=[dma((3,))],
+        compiler_params=pltpu.CompilerParams(vmem_limit_bytes=2**20),
+        name="deliver",
+    )(*results)
     return next_rows.reshape(1, nodes, hidden), node_loss.reshape(nodes), input_grad.reshape(1, nodes, f_in)
 
 

time: 82.1 us -> 80.3 us (0.978)
  local copies, waits for them, and re-layouts: 1.77 us -> 0 us
    unnamed x3 -> x0, local copies, waits for them, and re-layouts: 1.77 us -> none
where the time goes in v3:
time: 80.3 us; the launch traced here: 80.1 us
  Pallas kernels  79.5 us (99%)
    pallas_call x1, Pallas kernels, per_device(): pl.pallas_call(functools.partial(layer_kernel, wide, narrow), out_shape=(...  78.8 us

profile of v3, /device:TPU:1, one launch (start us, length us, event | category | flops | bytes accessed | tf_op | source)
XLA Modules:
  0.0 80.1 jit_solution(5612889592505684635)
XLA Ops:
  0.6 78.8 %layer.1 = (bf16[128,256]{1,0:T(8,128)(2,1)S(1)}, f32[1,128]{1,0:T(1,128)S(1)}, f32[128,128]{1,0:T(8,128)S(1)}) custom-call(bf16[128,128]{1,0:T(8,128)(2,1)} %bitcast.14, bf16[128,256]{1,0:T(8,128)(2,1)} %weight_hbm.1, f32[1,256]{1,0:T(1,128)} %bitcast.15, bf16[172,256]{1,0:T(8,128)(2,1)} %bitcast.13, bf16[96,128,128]{2,1,0:T(8,128)(2,1)} %bitcast.12, ...), custom_call_target="tpu_custom_call" | custom-call | tf_op jit(solution)/shard_map/layer/pallas_call | solution.py:487
  79.4 0.7 deliver.1

commit v4 on v3

--- a/solution.py
+++ b/solution.py
@@ -17,16 +17,24 @@
     ("x", 3), ("x", -3), ("x", 1), ("x", -1), ("own", 4), ("own", -4), ("own", 5), ("own", -5), ("own", 6),
     ("x", 2), ("x", -2), ("other", 4), ("other", -4), ("other", 5), ("other", -5), ("other", 6),
 )
+GROUPS = (
+    (0, 1), (1, 3), (3, 5), (5, 6), (6, 8), (8, 10), (10, 12), (12, 14), (14, 17), (17, 19), (19, 21), (21, 23), (23, 24),
+)
 SIBLING_LAG = 6
+
+
+def due(i):
+    return [p for p, (first, end) in enumerate(GROUPS) if end - 1 == i - SIBLING_LAG]
 
 
 def spread_order():
     order = []
     for i in range(len(ARRIVALS) + SIBLING_LAG):
-        for j, sibling in ((i, 0), (i - SIBLING_LAG, 1)):
-            if 0 <= j < len(ARRIVALS):
-                kind, offset = ARRIVALS[j]
-                order.append((int(kind != "own"), sibling, offset))
+        steps = [(i, 0)] if i < len(ARRIVALS) else []
+        steps += [(j, 1) for p in due(i) for j in range(*GROUPS[p])]
+        for j, sibling in steps:
+            kind, offset = ARRIVALS[j]
+            order.append((int(kind != "own"), sibling, offset))
     return order
 
 
@@ -72,10 +80,10 @@
     feat_hbm, weight_hbm, bias_hbm, cls_hbm, tiles_hbm, cols_hbm, counts_hbm, perm_hbm, labels_hbm,
     next_ref, loss_ref, grad_ref,
     feat, weight, bias, cls, tiles, cols, counts, perm, labels, table_v, table,
-    ft, sbuf, srecv, fbuf, frecv, xbuf, xrecv, zbuf, zrecv, own, gbuf, run,
+    ft, sbuf, srecv, fbuf, frecv, xbuf, xrecv, zbuf, zrecv, own, gbuf, gsib, run,
     pack, unpack, cxbuf, cxrecv, cybuf, cyrecv, cnbuf, cnrecv, cpad,
     in_sem, table_sem, fy_s, fy_r, fx_s, fx_r, s_s, s_r, f_s, f_r, x_s, x_r, z_s, z_r,
-    gz_s, gz_r, gx_s, gx_r, gs_s, gs_r, cx_s, cx_r, cy_s, cy_r, cn_s, cn_r, a_s, a_r,
+    g_s, g_r, gs_s, gs_r, cx_s, cx_r, cy_s, cy_r, cn_s, cn_r, a_s, a_r,
 ):
     Y, Z = wide // 2, narrow // 4
     w, n = lax.axis_index("wide"), lax.axis_index("narrow")
@@ -309,32 +317,31 @@
     grad_logits = shifted / exp_total - target.astype(f32)
     grad_act = split_dot(cls_t, grad_logits)
     grad_pre = (grad_act * gate_value * (1.0 + hidden_pre * (1.0 - gate_value))).astype(bf16)
-    gbuf[n] = dot(weight[...], grad_pre, (1, 0)).astype(bf16)
-
-    def gz(g, offset, slot, towards):
-        k = INWARD.index(offset)
-        return rcopy(gbuf.at[slot], gbuf.at[slot], gz_s.at[g, k], gz_r.at[g, k], z_dev(towards))
-
-    def gx(offset, slot):
-        k = INWARD.index(offset)
-        return rcopy(gbuf.at[slot], gbuf.at[slot], gx_s.at[k], gx_r.at[k], x_dev)
-
-    def gs(g, offset, slot):
-        k = INWARD.index(offset)
-        return rcopy(gbuf.at[slot], gbuf.at[slot], gs_s.at[g, k], gs_r.at[g, k], s_dev)
-
-    def pass_on(g, offset, slot):
+    gbuf[0] = dot(weight[...], grad_pre, (1, 0)).astype(bf16)
+
+    def hand(source, kind, offset, towards):
+        j = ARRIVALS.index((kind, offset))
+        device = x_dev if kind == "x" else z_dev(towards)
+        return rcopy(gbuf.at[source], gbuf.at[j], g_s.at[j], g_r.at[j], device)
+
+    def gs(p):
+        span = pl.ds(GROUPS[p][0], GROUPS[p][1] - GROUPS[p][0])
+        return rcopy(gbuf.at[span], gsib.at[span], gs_s.at[p], gs_r.at[p], s_dev)
+
+    def pass_on(j):
+        kind, offset = ARRIVALS[j]
+        into = "own" if kind == "own" else "other"
         if offset == -RELAY:
             for further, seen_at in ((3, 6), (2, -5), (1, -4)):
-                gz(g, seen_at, slot, further).start()
+                hand(j, into, seen_at, further).start()
         if offset == RELAY:
             for further, seen_at in ((-2, 5), (-1, 4)):
-                gz(g, seen_at, slot, further).start()
-
-    gx(0, n).start()
+                hand(j, into, seen_at, further).start()
+
+    hand(0, "x", 0, 0).start()
     for offset in (3, -3, 1, -1, 2, -2):
-        gz(0, -offset, n, offset).start()
-    gs(0, 0, n).start()
+        hand(0, "own", -offset, offset).start()
+    gs(0).start()
 
     pack[:, :hidden] = dot(chosen, activated, (1, 1)).astype(bf16)
 
@@ -353,9 +360,12 @@
 
     wait_forward()
 
-    def spread(b):
+    def spread(j, sibling):
+        kind, offset = ARRIVALS[j]
+        column_ = xh if kind == "own" else 1 - xh
+        b = nid(column_, zat(offset, -1), 1 - c) if sibling else nid(column_, zat(offset), c)
         right = jnp.concatenate([tiles[2 * b], tiles[2 * b + 1]], axis=1)
-        part = dot(gbuf[b], right, (1, 0))
+        part = dot(gsib[j] if sibling else gbuf[j], right, (1, 0))
         for t in range(2):
             run[2 * b + t + 1] = part[:, t * nodes : (t + 1) * nodes] + run[table[2 + t, b]]
 
@@ -363,43 +373,31 @@
     for i in range(len(ARRIVALS) + SIBLING_LAG):
         if i < len(ARRIVALS):
             kind, offset = ARRIVALS[i]
-            g = int(kind != "own")
-            slot = nid(xh if g == 0 else 1 - xh, zat(offset), c)
-            if kind == "x":
-                gx(offset, slot).wait_recv()
-                pass_on(1, offset, slot)
-                gs(1, offset, slot).start()
-            elif offset:
-                gz(g, offset, slot, 1).wait_recv()
-                if kind == "own":
-                    pass_on(0, offset, slot)
-                    if offset in NEAR:
-                        gx(offset, slot).start()
-                gs(g, offset, slot).start()
-            ready.append(slot)
-        if i >= SIBLING_LAG:
-            kind, offset = ARRIVALS[i - SIBLING_LAG]
-            g = int(kind != "own")
-            slot = nid(xh if g == 0 else 1 - xh, zat(offset, -1), 1 - c)
-            gs(g, offset, slot).wait_recv()
-            ready.append(slot)
+            if i:
+                hand(i, kind, offset, 1).wait_recv()
+                if kind != "other":
+                    pass_on(i)
+                if kind == "own" and offset in NEAR:
+                    hand(i, "x", offset, 0).start()
+                for p, (first, end) in enumerate(GROUPS):
+                    if end - 1 == i:
+                        gs(p).start()
+            ready.append((i, False))
+        for p in due(i):
+            gs(p).wait_recv()
+            ready += [(j, True) for j in range(*GROUPS[p])]
         if i % 4 == 3 or i == len(ARRIVALS) + SIBLING_LAG - 1:
-            for slot in ready:
-                spread(slot)
+            for j, sibling in ready:
+                spread(j, sibling)
             ready = []
 
     def wait_backward():
         for d in range(1, wide):
             a_copy(d, ring_step(w, d, wide), w).wait_send()
-        for offset in INWARD:
-            gs(0, offset, n).wait_send()
-            gs(1, offset, n).wait_send()
-            if offset in NEAR:
-                gx(offset, n).wait_send()
-            else:
-                gz(1, offset, n, 1).wait_send()
-            if offset:
-                gz(0, offset, n, 1).wait_send()
+        for j in range(1, len(ARRIVALS)):
+            hand(0, *ARRIVALS[j], 1).wait_send()
+        for p in range(len(GROUPS)):
+            gs(p).wait_send()
 
     def place():
         for d in range(1, wide):
@@ -515,7 +513,8 @@
             pltpu.VMEM((6,) + block, bf16),
             pltpu.VMEM((6,) + block, bf16),
             pltpu.VMEM((2, Z) + block, f32),
-            pltpu.VMEM((narrow,) + block, bf16),
+            pltpu.VMEM((len(ARRIVALS),) + block, bf16),
+            pltpu.VMEM((len(ARRIVALS),) + block, bf16),
             pltpu.VMEM((narrow * 2 + 1,) + block, f32),
             pltpu.VMEM((wide * slots, hidden + nodes), bf16),
             pltpu.VMEM((wide * slots, hidden + nodes), bf16),
@@ -529,7 +528,7 @@
             dma((9,)), dma,
             dma((Y - 1,)), dma((Y - 1,)), dma((Y,)), dma((Y,)),
             dma((2, 2)), dma((2, 2)), dma((2, 5)), dma((2, 5)), dma((2,)), dma((2,)), dma((6,)), dma((6,)),
-            dma((2, Z)), dma((2, Z)), dma((Z,)), dma((Z,)), dma((2, Z)), dma((2, Z)),
+            dma((len(ARRIVALS),)), dma((len(ARRIVALS),)), dma((len(GROUPS),)), dma((len(GROUPS),)),
             dma((4,)), dma((4,)), dma((3,)), dma((3,)), dma((2, 4)), dma((2, 4)), dma((wide,)), dma((wide,)),
         ],
         compiler_params=pltpu.CompilerParams(

time: 80.3 us -> 78.1 us (0.973)
  Pallas kernels: 79.5 us -> 77 us
    pallas_call x1, Pallas kernels: 78.8 us -> 76.3 us  [per_device(): pl.pallas_call(functools.partial(layer_kernel, wide, narrow), out_shape=(...]
where the time goes in v4:
time: 78.1 us; the launch traced here: 77.7 us
  Pallas kernels  77 us (99%)
    pallas_call x1, Pallas kernels, per_device(): pl.pallas_call(functools.partial(layer_kernel, wide, narrow), out_shape=(...  76.3 us

profile of v4, /device:TPU:1, one launch (start us, length us, event | category | flops | bytes accessed | tf_op | source)
XLA Modules:
  0.0 77.7 jit_solution(9574204651637930500)
XLA Ops:
  0.6 76.3 %layer.1 = (bf16[128,256]{1,0:T(8,128)(2,1)S(1)}, f32[1,128]{1,0:T(1,128)S(1)}, f32[128,128]{1,0:T(8,128)S(1)}) custom-call(bf16[128,128]{1,0:T(8,128)(2,1)} %bitcast.14, bf16[128,256]{1,0:T(8,128)(2,1)} %weight_hbm.1, f32[1,256]{1,0:T(1,128)} %bitcast.15, bf16[172,256]{1,0:T(8,128)(2,1)} %bitcast.13, bf16[96,128,128]{2,1,0:T(8,128)(2,1)} %bitcast.12, ...), custom_call_target="tpu_custom_call" | custom-call | tf_op jit(solution)/shard_map/layer/pallas_call | solution.py:485
  77.0 0.7 deliver.1
